TPU v7x, 512 devices: a whole 4x8x8 slice. The times are simulated.
512 devices in a mesh: leaf: 4 (over x), row: 16 (over z, core), col: 8 (over y).
Axes of the slice: x: 4, y: 8, z: 8, core: 2. Of those that a mesh axis runs over, the one named last changes fastest.
Arguments:
- widths: int32 [15], replicated, may hold values from 1024 to 2048, as said below
- bottom_lists: int32 [8, 32], P('leaf'), may hold values from 0 to 47, as said below
- root_inverse: bfloat16 [2048, 2048], P('row')
- second_panels: bfloat16 [4, 2048, 1024], P('leaf', 'row', 'col'), may hold values from -0.09375 to 0.09375
- second_inverse: bfloat16 [4, 1024, 2048], P('leaf', 'col', 'row')
- third_panels: bfloat16 [4, 2, 2048, 2048], P('leaf', None, 'row', 'col'), may hold values from -0.09375 to 0.09375
- third_inverse: bfloat16 [4, 2048, 2048], P('leaf', 'col', 'row')
- bottom_panels: bfloat16 [8, 4096, 2048], P('leaf', 'row', 'col'), may hold values from -0.09375 to 0.09375
- bottom_inverse: bfloat16 [8, 2048, 2048], P('leaf', 'col', 'row')
Outputs:
- second_off: bfloat16 [4, 2048, 1024], P('leaf', 'row', 'col')
- second_diag: bfloat16 [4, 1024, 2048], P('leaf', 'col', 'row')
- third_off: bfloat16 [4, 2, 2048, 2048], P('leaf', None, 'row', 'col')
- third_diag: bfloat16 [4, 2048, 2048], P('leaf', 'col', 'row')
- bottom_off: bfloat16 [8, 3, 2048, 2048], P('leaf', None, 'row', 'col')
- bottom_diag: bfloat16 [8, 2048, 2048], P('leaf', 'col', 'row')
Inputs may be any that keep to these rules, and one draw needn't show every extreme that they name: `widths`: some supernode has 2048 columns and some 2048/2. `bottom_lists`: row e lists 32 different blocks of 128 rows of its chain (root, then second-level ancestor, then parent, 16 blocks each) in increasing order; block 0 and all blocks of the parent are always listed.
All inputs are finite; a program needn't handle non-finite values.
Results may differ from a plain program's by a relative error of at most 0.015.
Values may be sent and summed in bfloat16 or wider, within the bound.
A program may use at most 64 MiB of HBM per device.

v0:
```python
import jax
import jax.numpy as jnp
from jax import lax
from jax.sharding import PartitionSpec as P

NODES = 15
BOTTOM = 8


def partner(block, axis, apart):
    count = lax.axis_size(axis)
    route = []
    for low in range(count):
        high = low | 1 << apart
        if high != low and high < count:
            route += [(low, high), (high, low)]
    return lax.ppermute(block, axis, route)


def node_width(widths, node_at):
    return jnp.sum(jnp.where(jnp.arange(widths.shape[0]) == node_at, widths, 0))


def chain_fold(flat_chain, tile_width, ancestors, shard_piece):
    piece_rows = shard_piece.shape[1]
    picked = jnp.concatenate(
        [
            lax.dynamic_slice_in_dim(flat_chain, level_at * tile_width, piece_rows, 1)
            for level_at in range(ancestors)
        ],
        axis=1,
    )
    stacked = shard_piece.reshape(ancestors * piece_rows, shard_piece.shape[2])
    return jnp.dot(picked, stacked, preferred_element_type=jnp.float32)


def local(
    widths,
    bottom_lists,
    root_inverse,
    second_panels,
    second_inverse,
    third_panels,
    third_inverse,
    bottom_panels,
    bottom_inverse,
):
    group_at = lax.axis_index("leaf")
    row_at = lax.axis_index("row")
    col_at = lax.axis_index("col")
    rows_dev = root_inverse.shape[0]
    tile_width = root_inverse.shape[1]
    half_cols = second_panels.shape[2]
    own_cols = third_panels.shape[3]
    half_at = group_at % 2
    parent_one = 1 + group_at // 2
    node_two = 3 + group_at
    row_first = row_at * rows_dev
    row_index = row_first + jnp.arange(rows_dev)
    root_width = node_width(widths, 0)
    root_mask = (row_index < root_width)[:, None] & (jnp.arange(tile_width) < root_width)[None, :]
    root_block = jnp.where(root_mask, root_inverse, 0)
    width_one = node_width(widths, parent_one)
    mask_rows_one = row_index < width_one
    first_col = half_at * (tile_width // 2) + col_at * half_cols
    mask_cols_one = first_col + jnp.arange(half_cols) < width_one
    panel_one = jnp.where(mask_cols_one[None, :], second_panels[0], 0)
    flat_piece = lax.all_gather(panel_one, "row", axis=0, tiled=True)
    product_one = jnp.dot(root_block, flat_piece, preferred_element_type=jnp.float32)
    off_one = (-product_one).astype(jnp.bfloat16)
    mine_half = lax.all_gather(off_one, "col", axis=1, tiled=True)
    other_half = partner(mine_half, "leaf", 0)
    off_full = jnp.where(
        half_at == 0,
        jnp.concatenate([mine_half, other_half], 1),
        jnp.concatenate([other_half, mine_half], 1),
    )
    term_one = lax.dot_general(
        panel_one, off_full, (((0,), (0,)), ((), ())), preferred_element_type=jnp.float32
    )
    summed_one = lax.psum_scatter(
        term_one.astype(jnp.bfloat16), "row", scatter_dimension=1, tiled=True
    ).astype(jnp.float32)
    inverse_one = jnp.where(
        mask_cols_one[:, None] & mask_rows_one[None, :], second_inverse[0], 0
    ).astype(jnp.float32)
    diag_one = (inverse_one - summed_one).astype(jnp.bfloat16)
    mine_diag = lax.all_gather(diag_one.T, "col", axis=1, tiled=True)
    other_diag = partner(mine_diag, "leaf", 0)
    diag_full = jnp.where(
        half_at == 0,
        jnp.concatenate([mine_diag, other_diag], 1),
        jnp.concatenate([other_diag, mine_diag], 1),
    )
    second_off = off_one[None]
    second_diag = diag_one[None]
    turned_one = lax.all_to_all(off_full, "row", split_axis=1, concat_axis=0, tiled=True)
    chain_two = jnp.stack(
        [jnp.concatenate([root_block, off_full], 1), jnp.concatenate([turned_one.T, diag_full], 1)],
        0,
    )
    flat_two = chain_two.reshape(2 * rows_dev, 2 * tile_width)
    first_own = col_at * own_cols
    width_two = node_width(widths, node_two)
    mask_cols_two = first_own + jnp.arange(own_cols) < width_two
    panel_two = jnp.where(mask_cols_two[None, None, :], third_panels[0], 0)
    product_two = chain_fold(
        flat_two, tile_width, 2, lax.all_gather(panel_two, "row", axis=1, tiled=True)
    )
    off_two = (-product_two).astype(jnp.bfloat16).reshape(2, rows_dev, own_cols)
    full_two = lax.all_gather(off_two, "col", axis=2, tiled=True)
    term_two = jnp.einsum("kin,kim->nm", panel_two, full_two, preferred_element_type=jnp.float32)
    summed_two = lax.psum_scatter(
        term_two.astype(jnp.bfloat16), "row", scatter_dimension=1, tiled=True
    ).astype(jnp.float32)
    mask_rows_two = row_index < width_two
    inverse_two = jnp.where(
        mask_cols_two[:, None] & mask_rows_two[None, :], third_inverse[0], 0
    ).astype(jnp.float32)
    diag_two = (inverse_two - summed_two).astype(jnp.bfloat16)
    diag_rows_two = lax.all_gather(diag_two.T, "col", axis=1, tiled=True)
    turned_two = lax.all_to_all(full_two, "row", split_axis=2, concat_axis=1, tiled=True)
    lower_two = jnp.transpose(turned_two, (2, 0, 1)).reshape(rows_dev, 2 * tile_width)
    chain_three = jnp.stack(
        [
            jnp.concatenate([chain_two[0], full_two[0]], 1),
            jnp.concatenate([chain_two[1], full_two[1]], 1),
            jnp.concatenate([lower_two, diag_rows_two], 1),
        ],
        0,
    )
    flat_three = chain_three.reshape(3 * rows_dev, 3 * tile_width)
    bottom_dev = bottom_panels.shape[0]
    list_len = bottom_lists.shape[1]
    block_rows = 2 * tile_width // list_len
    node_three = NODES - BOTTOM + bottom_dev * group_at + jnp.arange(bottom_dev)
    width_three = jnp.sum(
        jnp.where(jnp.arange(widths.shape[0])[None, :] == node_three[:, None], widths[None, :], 0),
        1,
    )
    mask_cols_three = (first_own + jnp.arange(own_cols))[None, :] < width_three[:, None]
    panel_three = jnp.where(mask_cols_three[:, None, :], bottom_panels, 0)
    positions = (
        jnp.repeat(bottom_lists, block_rows, axis=1) * block_rows
        + jnp.arange(list_len * block_rows) % block_rows
    )
    own_chain = (jnp.arange(3)[:, None] * tile_width + row_index[None, :]).reshape(-1)
    matches = bottom_lists[:, :, None] == (own_chain // block_rows)[None, None, :]
    member = jnp.any(matches, axis=1)
    lower_all = lax.all_gather(panel_three, "row", axis=1, tiled=True)
    spread = jax.vmap(
        lambda where_to, values_in: jnp.zeros((3 * tile_width, own_cols), jnp.bfloat16)
        .at[where_to]
        .set(values_in)
    )(positions, lower_all)
    product_three = jnp.einsum(
        "ab,ebn->ean", flat_three, spread, preferred_element_type=jnp.float32
    )
    chain_rows = lax.dynamic_slice_in_dim(
        spread.reshape(bottom_dev, 3, tile_width, own_cols), row_first, rows_dev, 2
    )
    off_three = jnp.where(member[:, :, None], -product_three, 0.0).astype(jnp.bfloat16)
    off_three = off_three.reshape(bottom_dev, 3, rows_dev, own_cols)
    full_three = lax.all_gather(off_three, "col", axis=3, tiled=True)
    term_three = jnp.einsum(
        "ekin,ekim->enm", chain_rows, full_three, preferred_element_type=jnp.float32
    )
    summed_three = lax.psum_scatter(
        term_three.astype(jnp.bfloat16), "row", scatter_dimension=2, tiled=True
    ).astype(jnp.float32)
    mask_rows_three = row_index[None, :] < width_three[:, None]
    inverse_three = jnp.where(
        mask_cols_three[:, :, None] & mask_rows_three[:, None, :], bottom_inverse, 0
    ).astype(jnp.float32)
    diag_three = (inverse_three - summed_three).astype(jnp.bfloat16)
    return (second_off, second_diag, off_two[None], diag_two[None], off_three, diag_three)


def solution(mesh):
    in_specs = (
        P(),
        P("leaf", None),
        P("row", None),
        P("leaf", "row", "col"),
        P("leaf", "col", "row"),
        P("leaf", None, "row", "col"),
        P("leaf", "col", "row"),
        P("leaf", "row", "col"),
        P("leaf", "col", "row"),
    )
    out_specs = (
        P("leaf", "row", "col"),
        P("leaf", "col", "row"),
        P("leaf", None, "row", "col"),
        P("leaf", "col", "row"),
        P("leaf", None, "row", "col"),
        P("leaf", "col", "row"),
    )
    return jax.shard_map(local, mesh=mesh, in_specs=in_specs, out_specs=out_specs, check_vma=False)
```

profile of v0, /device:TPU:8, one launch (start us, length us, event | category | flops | bytes accessed | tf_op | source)
XLA Modules:
  0.0 519.0 jit_solution(5305973732029650270)
XLA Ops:
  7.2 0.9 copy.58
  8.1 1.3 fusion.20
  9.5 0.7 add_compare_fusion
  10.2 24.6 %all_gather.24 = bf16[2048,128]{0,1:T(8,128)(2,1)S(1)} all-gather(bf16[128,128]{0,1:T(8,128)(2,1)S(1)} %bitcast_select_fusion.1), channel_id=1, replica_groups=mesh['leaf'=4,'row'=16,'col'=8] {'row'}, dimensions={0}, use_global_device_ids=true | all-gather | bytes 557056 | tf_op jit(solution)/shard_map/all_gather | solution.py:68
  34.8 0.7 iota_compare_fusion
  35.5 0.7 broadcast_compare_fusion.5
  36.1 1.3 and_select_fusion
  37.4 0.3 fusion.7
  37.7 23.5 %all_gather.25 = bf16[128,1024]{1,0:T(8,128)(2,1)S(1)} all-gather(bf16[128,128]{1,0:T(8,128)(2,1)S(1)} %fusion.7), channel_id=1, replica_groups=mesh['leaf'=4,'row'=16,'col'=8] {'col'}, dimensions={1}, use_global_device_ids=true | all-gather | bytes 294912 | tf_op jit(solution)/shard_map/all_gather | solution.py:71
  61.3 3.5 collective-permute-start
  64.8 4.9 collective-permute-done
  69.6 0.1 maximum_select_fusion
  69.8 1.2 convolution_convert_fusion
  71.0 0.7 broadcast_compare_fusion.2
  71.7 0.7 bitcast_select_fusion
  72.5 0.9 maximum_select_fusion.1
  73.4 3.6 all-to-all-start
  77.0 0.1 copy.59
  77.1 0.7 broadcast_compare_fusion.4
  77.8 49.9 %reduce-scatter.6.cloned.1.call-done = bf16[128,128]{0,1:T(8,128)(2,1)} async-done(((bf16[128,2048]{0,1:T(8,128)(2,1)}), bf16[128,128]{0,1:T(8,128)(2,1)}) %reduce-scatter.6.cloned.1.call-update) | async-done | bytes 32784 | tf_op jit(solution)/shard_map/reduce_scatter | solution.py:81
  127.7 0.8 fusion.22
  128.6 23.1 %all_gather.26 = bf16[128,1024]{1,0:T(8,128)(2,1)S(1)} all-gather(bf16[128,128]{1,0:T(8,128)(2,1)S(1)} %get-tuple-element.37), channel_id=1, replica_groups=mesh['leaf'=4,'row'=16,'col'=8] {'col'}, dimensions={1}, use_global_device_ids=true | all-gather | bytes 294912 | tf_op jit(solution)/shard_map/all_gather | solution.py:88
  151.7 3.2 collective-permute-start.1
  154.9 0.1 maximum_bitcast_fusion.3
  155.0 0.2 copy.81
  155.2 4.8 collective-permute-done.1
  160.0 1.2 maximum_select_fusion.2
  161.3 1.5 pad_maximum_fusion.1
  162.8 9.9 %all-gather.5.cloned.1.call-done = bf16[2,2048,256]{2,1,0:T(8,128)(2,1)} async-done(((bf16[2,128,256]{2,1,0:T(8,128)(2,1)}), bf16[2,2048,256]{2,1,0:T(8,128)(2,1)}) %all-gather.5.cloned.1.call-update) | async-done | bytes 2097168 | tf_op jit(solution)/shard_map/all_gather | solution.py:108
  172.8 3.6 fusion.6
  176.5 39.9 %all-gather.7.cloned.1.call-done = bf16[2,128,2048]{2,1,0:T(8,128)(2,1)} async-done(((bf16[2,128,256]{2,1,0:T(8,128)(2,1)}), bf16[2,128,2048]{2,1,0:T(8,128)(2,1)}) %all-gather.7.cloned.1.call-update) | async-done | bytes 1048592 | tf_op jit(solution)/shard_map/all_gather | solution.py:111
  216.4 2.8 fusion.2
  219.4 0.2 fusion.17
  219.6 0.7 broadcast_select_fusion
  220.6 0.1 multiply_reduce_fusion
  220.7 0.1 and_reduce_fusion
  220.8 2.0 copy.69
  222.8 7.5 %all-to-all-start.1 = ((bf16[2,128,2048]{1,0,2:T(2,128)(2,1)}), bf16[2,128,2048]{1,0,2:T(2,128)(2,1)}, u32[]{:S(2)}, u32[]{:S(2)}) async-start(bf16[2,128,2048]{1,0,2:T(2,128)(2,1)} %copy.69), calls=%async_computation.3 | async-start | bytes 2097152 | tf_op jit(solution)/shard_map/all_to_all | solution.py:122
  230.5 0.1 copy.66
  230.6 0.7 broadcast_compare_fusion.3
  231.4 0.1 compare_reduce_fusion
  231.5 2.3 maximum_bitcast_fusion
  233.8 24.9 %all-to-all-done.1 = bf16[2,128,2048]{1,0,2:T(2,128)(2,1)} async-done(((bf16[2,128,2048]{1,0,2:T(2,128)(2,1)}), bf16[2,128,2048]{1,0,2:T(2,128)(2,1)}, u32[]{:S(2)}, u32[]{:S(2)}) %all-to-all-start.1) | async-done | bytes 1048608 | tf_op jit(solution)/shard_map/all_to_all | solution.py:122
  258.8 1.9 copy.95
  260.7 0.4 copy.90
  261.1 25.3 %reduce-scatter.8.cloned.1.call-done = bf16[256,128]{0,1:T(8,128)(2,1)} async-done(((bf16[256,2048]{0,1:T(8,128)(2,1)}), bf16[256,128]{0,1:T(8,128)(2,1)}) %reduce-scatter.8.cloned.1.call-update) | async-done | bytes 65552 | tf_op jit(solution)/shard_map/reduce_scatter | solution.py:113
  286.4 0.9 fusion.24
  287.3 25.9 %all_gather.30 = bf16[128,2048]{1,0:T(8,128)(2,1)S(1)} all-gather(bf16[128,256]{1,0:T(8,128)(2,1)S(1)} %get-tuple-element.35), channel_id=1, replica_groups=mesh['leaf'=4,'row'=16,'col'=8] {'col'}, dimensions={1}, use_global_device_ids=true | all-gather | bytes 589824 | tf_op jit(solution)/shard_map/all_gather | solution.py:121
  313.2 0.1 maximum_bitcast_fusion.2
  313.3 3.6 pad_maximum_fusion
  317.0 18.1 %all-gather.9.cloned.1.call-done = bf16[2,4096,256]{2,1,0:T(8,128)(2,1)} async-done(((bf16[2,256,256]{2,1,0:T(8,128)(2,1)}), bf16[2,4096,256]{2,1,0:T(8,128)(2,1)}) %all-gather.9.cloned.1.call-update) | async-done | bytes 4194320 | tf_op jit(solution)/shard_map/all_gather | solution.py:150
  335.1 39.1 %scatter_custom_fusion = bf16[12288,256]{1,0:T(8,128)(2,1)} fusion(s32[8192]{0:T(1024)S(1)} %bitcast.140, bf16[8192,256]{1,0:T(8,128)(2,1)} %bitcast.141, bf16[]{:T(256)} %constant.73.clone.1), kind=kCustom, calls=%fused_computation.3 | custom fusion | bytes 6291968
  374.1 7.6 %fusion.5 = bf16[2,384,256]{1,2,0:T(8,128)(2,1)S(1)} fusion(bf16[2,6144,256]{2,1,0:T(8,128)(2,1)} %bitcast.125, bf16[384,6144,1]{1,0,2:T(8,128)(2,1)} %bitcast.127, pred[2,384]{1,0:T(4,128)(4,1)S(1)} %compare_reduce_fusion), kind=kOutput, calls=%fused_computation.15 | convolution fusion | flops 2416508928 | bytes 11404032 | tf_op jit(solution)/shard_map/ab,ebn->ean/dot_general | solution.py:156
  381.7 0.9 copy.72
  382.7 57.5 %all-gather.11.cloned.1.call-done = bf16[2,3,128,2048]{3,2,1,0:T(8,128)(2,1)} async-done(((bf16[2,3,128,256]{3,2,1,0:T(8,128)(2,1)}), bf16[2,3,128,2048]{3,2,1,0:T(8,128)(2,1)}) %all-gather.11.cloned.1.call-update) | async-done | bytes 3145744 | tf_op jit(solution)/shard_map/all_gather | solution.py:164
  440.2 3.3 bitcast_convert_fusion
  443.6 3.8 copy.83
  447.4 3.4 copy.91
  450.9 0.7 copy.74
  451.6 0.7 copy.75
  452.3 57.9 %reduce-scatter.10.cloned.1.call-done = bf16[128,512]{1,0:T(8,128)(2,1)} async-done(((bf16[2048,512]{1,0:T(8,128)(2,1)}), bf16[128,512]{1,0:T(8,128)(2,1)}) %reduce-scatter.10.cloned.1.call-update) | async-done | bytes 131088
  510.3 0.9 reshape.268
  511.2 0.1 copy.84
  511.4 0.8 subtract_convert_fusion
  (61 shorter events, 1.2 us)
Async XLA Ops:
  7.2 64.5 %copy-start.5 = (bf16[1,2,128,256]{3,2,1,0:T(8,128)(2,1)S(1)}, bf16[1,2,128,256]{3,2,1,0:T(8,128)(2,1)}, u32[]{:S(2)}) copy-start(bf16[1,2,128,256]{3,2,1,0:T(8,128)(2,1)} %param.14) | copy-start | bytes 393220
  7.2 120.6 %reduce-scatter.6.cloned.1.call-start = ((), (), s32[]{:S(2)}) async-start(), calls=%async_computation.5 | async-start | bytes 557056 | tf_op jit(solution)/shard_map/reduce_scatter | solution.py:81
  37.7 35.7 %copy-start.4 = (bf16[128,128]{1,0:T(8,128)(2,1)}, bf16[128,128]{1,0:T(8,128)(2,1)S(1)}, u32[]{:S(2)}) copy-start(bf16[128,128]{1,0:T(8,128)(2,1)S(1)} %fusion.7) | copy-start | bytes 98308
  61.3 15.8 %copy-start.8 = (bf16[1,128,128]{2,1,0:T(8,128)(2,1)S(1)}, bf16[1,128,128]{2,1,0:T(8,128)(2,1)}, u32[]{:S(2)}) copy-start(bf16[1,128,128]{2,1,0:T(8,128)(2,1)} %param.13) | copy-start | bytes 98308
  61.3 8.4 %collective-permute-start = (bf16[128,1024]{1,0:T(8,128)(2,1)S(1)}, bf16[128,1024]{1,0:T(8,128)(2,1)S(1)}, u32[]{:S(2)}, u32[]{:S(2)}) collective-permute-start(bf16[128,1024]{1,0:T(8,128)(2,1)S(1)} %all_gather.25), channel_id=1, source_target_pairs={{0,128},{128,0},{256,384},{384,256},{1,129},{129,1},{257,385},{385... | collective-permute-start | bytes 786440 | tf_op jit(solution)/shard_map/ppermute | solution.py:17
  71.0 101.8 %all-gather.5.cloned.1.call-start = ((), (), s32[]{:S(2)}) async-start(), calls=%async_computation.6 | async-start | bytes 2228224 | tf_op jit(solution)/shard_map/all_gather | solution.py:108
  73.4 81.6 %all-to-all-start = ((bf16[128,16,128]{2,0,1:T(8,128)(2,1)}), bf16[128,16,128]{2,0,1:T(8,128)(2,1)S(1)}, u32[]{:S(2)}, u32[]{:S(2)}) async-start(bf16[128,16,128]{2,0,1:T(8,128)(2,1)} %maximum_select_fusion.1), calls=%async_computation.1 | async-start | bytes 1048576 | tf_op jit(solution)/shard_map/all_to_all | solution.py:97
  77.0 139.4 %all-gather.7.cloned.1.call-start = ((), (), s32[]{:S(2)}) async-start(), calls=%async_computation.7 | async-start | bytes 1179648 | tf_op jit(solution)/shard_map/all_gather | solution.py:111
  151.7 8.4 %collective-permute-start.1 = (bf16[128,1024]{1,0:T(8,128)(2,1)S(1)}, bf16[128,1024]{1,0:T(8,128)(2,1)}, u32[]{:S(2)}, u32[]{:S(2)}) collective-permute-start(bf16[128,1024]{1,0:T(8,128)(2,1)S(1)} %all_gather.26), channel_id=1, source_target_pairs={{0,128},{128,0},{256,384},{384,256},{1,129},{129,1},{257,385},{385... | collective-permute-start | bytes 786440 | tf_op jit(solution)/shard_map/ppermute | solution.py:17
  161.2 1.6 copy-start.1
  162.8 53.6 %copy-start.2 = (bf16[2,128,256]{2,1,0:T(8,128)(2,1)S(1)}, bf16[2,128,256]{2,1,0:T(8,128)(2,1)}, u32[]{:S(2)}) copy-start(bf16[2,128,256]{2,1,0:T(8,128)(2,1)} %bitcast_select_fusion) | copy-start | bytes 393220
  172.8 46.6 %copy-start.12 = (s32[15]{0:T(128)S(1)}, s32[15]{0:T(128)}, u32[]{:S(2)}) copy-start(s32[15]{0:T(128)} %param.9) | copy-start | bytes 184
  172.8 46.9 %copy-start.3 = (bf16[2,256,256]{2,1,0:T(8,128)(2,1)S(1)}, bf16[2,256,256]{2,1,0:T(8,128)(2,1)}, u32[]{:S(2)}) copy-start(bf16[2,256,256]{2,1,0:T(8,128)(2,1)} %param.16) | copy-start | bytes 786436
  176.4 44.0 %copy-start.9 = (s32[2,32]{1,0:T(2,128)S(1)}, s32[2,32]{1,0:T(2,128)}, u32[]{:S(2)}) copy-start(s32[2,32]{1,0:T(2,128)} %param.10) | copy-start | bytes 772
  176.4 44.2 %copy-start.11 = (s32[2]{0:T(128)S(1)}, s32[2]{0:T(128)}, u32[]{:S(2)}) copy-start(s32[2]{0:T(128)} %constant.94) | copy-start | bytes 28
  176.4 44.3 %copy-start.10 = (s32[2]{0:T(128)S(1)}, s32[2]{0:T(128)}, u32[]{:S(2)}) copy-start(s32[2]{0:T(128)} %constant.97) | copy-start | bytes 28
  176.4 110.0 %reduce-scatter.8.cloned.1.call-start = ((), (), s32[]{:S(2)}) async-start(), calls=%async_computation.8 | async-start | bytes 1114112 | tf_op jit(solution)/shard_map/reduce_scatter | solution.py:113
  216.4 4.4 copy-start
  219.2 11.2 %copy-start.7 = (bf16[1,256,128]{2,1,0:T(8,128)(2,1)S(1)}, bf16[1,256,128]{2,1,0:T(8,128)(2,1)}, u32[]{:S(2)}) copy-start(bf16[1,256,128]{2,1,0:T(8,128)(2,1)} %param.15) | copy-start | bytes 196612
  219.3 115.8 %all-gather.9.cloned.1.call-start = ((), (), s32[]{:S(2)}) async-start(), calls=%async_computation.9 | async-start | bytes 4456448 | tf_op jit(solution)/shard_map/all_gather | solution.py:150
  222.8 35.9 %all-to-all-start.1 = ((bf16[2,128,2048]{1,0,2:T(2,128)(2,1)}), bf16[2,128,2048]{1,0,2:T(2,128)(2,1)}, u32[]{:S(2)}, u32[]{:S(2)}) async-start(bf16[2,128,2048]{1,0,2:T(2,128)(2,1)} %copy.69), calls=%async_computation.3 | async-start | bytes 2097152 | tf_op jit(solution)/shard_map/all_to_all | solution.py:122
  230.4 209.9 %all-gather.11.cloned.1.call-start = ((), (), s32[]{:S(2)}) async-start(), calls=%async_computation.10 | async-start | bytes 3538944 | tf_op jit(solution)/shard_map/all_gather | solution.py:164
  382.7 127.6 %reduce-scatter.10.cloned.1.call-start = ((), (), s32[]{:S(2)}) async-start(), calls=%async_computation.11 | async-start | bytes 2228224
  447.4 64.0 %copy-start.6 = (bf16[2,256,128]{2,1,0:T(8,128)(2,1)S(1)}, bf16[2,256,128]{2,1,0:T(8,128)(2,1)}, u32[]{:S(2)}) copy-start(bf16[2,256,128]{2,1,0:T(8,128)(2,1)} %param.17) | copy-start | bytes 393220
Sparse Core Ops, SparseCore 0:
  71.1 56.6 reduce-scatter.5
  130.7 42.0 all-gather.4
  176.5 39.8 all-gather.6
  219.4 66.9 reduce-scatter.7
  288.9 46.0 all-gather.8
  382.8 57.3 all-gather.10
  450.9 59.3 reduce-scatter.9
where the time goes:
time: 520 us; the launch traced here: 519 us
  waiting for transfers between devices  293 us (56%)
  blocking collectives  97.1 us (19%)
  local copies, waits for them, and re-layouts  55.7 us (11%)
  other arithmetic  21.3 us (4%)
  matrix products  18.9 us (4%)
  starting transfers between devices  18.1 us (3%)
  between operations  14.6 us (3%)
    unnamed x8, waiting for transfers between devices  58.1 us
    all_gather x1, waiting for transfers between devices, local(): full_three = lax.all_gather(off_three, 'col', axis=3, tiled=True)  57.5 us
    unnamed x39, local copies, waits for them, and re-layouts  50.3 us
    reduce_scatter x1, waiting for transfers between devices, local(): lax.psum_scatter(term_one.astype(jnp.bfloat16), 'row', scatter_dimension=...  49.9 us
    all_gather x1, waiting for transfers between devices, local(): full_two = lax.all_gather(off_two, 'col', axis=2, tiled=True)  39.9 us
    all_gather x1, blocking collectives, local(): diag_rows_two = lax.all_gather(diag_two.T, 'col', axis=1, tiled=True)  25.9 us
    reduce_scatter x1, waiting for transfers between devices, local(): lax.psum_scatter(term_two.astype(jnp.bfloat16), 'row', scatter_dimension=...  25.3 us
    all_to_all x1, waiting for transfers between devices, local(): lax.all_to_all(full_two, 'row', split_axis=2, concat_axis=1, tiled=True)  24.9 us
  transfers between devices with their start and end apart: 11, of which 10 were waited for; matrix products, arithmetic and copies ran while one was open for 4% of the time, Pallas kernels for 0%

commit v1 on v0

--- a/solution.py
+++ b/solution.py
@@ -119,7 +119,10 @@
     ).astype(jnp.float32)
     diag_two = (inverse_two - summed_two).astype(jnp.bfloat16)
     diag_rows_two = lax.all_gather(diag_two.T, "col", axis=1, tiled=True)
-    turned_two = lax.all_to_all(full_two, "row", split_axis=2, concat_axis=1, tiled=True)
+    turned_two = jnp.concatenate(
+        lax.all_to_all(jnp.stack(jnp.split(full_two, lax.axis_size("row"), axis=2)), "row", 0, 0),
+        axis=1,
+    )
     lower_two = jnp.transpose(turned_two, (2, 0, 1)).reshape(rows_dev, 2 * tile_width)
     chain_three = jnp.stack(
         [

time: 520 us -> 523 us (level)
  the two profiles are of different devices: /device:TPU:8 before, /device:TPU:2 now
where the time goes in v1:
time: 523 us; the launch traced here: 522 us
  waiting for transfers between devices  282 us (54%)
  blocking collectives  101 us (19%)
  local copies, waits for them, and re-layouts  66.1 us (13%)
  other arithmetic  22.4 us (4%)
  matrix products  18.9 us (4%)
  starting transfers between devices  16.5 us (3%)
  between operations  14.6 us (3%)
    unnamed x8, waiting for transfers between devices  60.1 us
    unnamed x53, local copies, waits for them, and re-layouts  59.5 us
    all_gather x1, waiting for transfers between devices, local(): full_three = lax.all_gather(off_three, 'col', axis=3, tiled=True)  55.5 us
    reduce_scatter x1, waiting for transfers between devices, local(): lax.psum_scatter(term_one.astype(jnp.bfloat16), 'row', scatter_dimension=...  48.9 us
    all_gather x1, waiting for transfers between devices, local(): full_two = lax.all_gather(off_two, 'col', axis=2, tiled=True)  39.9 us
    all_gather x1, blocking collectives, local(): diag_rows_two = lax.all_gather(diag_two.T, 'col', axis=1, tiled=True)  27.5 us
    all_to_all x1, waiting for transfers between devices, local(): lax.all_to_all(jnp.stack(jnp.split(full_two, lax.axis_size('row'), axis=2...  25.5 us
    all_gather x1, blocking collectives, local(): mine_half = lax.all_gather(off_one, 'col', axis=1, tiled=True)  25 us
  transfers between devices with their start and end apart: 11, of which 10 were waited for; matrix products, arithmetic and copies ran while one was open for 6% of the time, Pallas kernels for 0%

profile of v1, /device:TPU:2, one launch (start us, length us, event | category | flops | bytes accessed | tf_op | source)
XLA Modules:
  0.0 521.7 jit_solution(13412036987379010157)
XLA Ops:
  7.2 0.9 copy.58
  8.1 1.3 fusion.36
  9.5 0.7 add_compare_fusion
  10.2 24.6 %all_gather.24 = bf16[2048,128]{0,1:T(8,128)(2,1)S(1)} all-gather(bf16[128,128]{0,1:T(8,128)(2,1)S(1)} %bitcast_select_fusion.1), channel_id=1, replica_groups=mesh['leaf'=4,'row'=16,'col'=8] {'row'}, dimensions={0}, use_global_device_ids=true | all-gather | bytes 557056 | tf_op jit(solution)/shard_map/all_gather | solution.py:68
  34.8 0.7 iota_compare_fusion
  35.5 0.7 broadcast_compare_fusion.5
  36.1 1.3 and_select_fusion
  37.7 25.0 %all_gather.25 = bf16[128,1024]{1,0:T(8,128)(2,1)S(1)} all-gather(bf16[128,128]{1,0:T(8,128)(2,1)S(1)} %fusion.7), channel_id=1, replica_groups=mesh['leaf'=4,'row'=16,'col'=8] {'col'}, dimensions={1}, use_global_device_ids=true | all-gather | bytes 294912 | tf_op jit(solution)/shard_map/all_gather | solution.py:71
  62.7 2.6 collective-permute-start
  65.3 5.8 %collective-permute-done = bf16[128,1024]{1,0:T(8,128)(2,1)S(1)} collective-permute-done((bf16[128,1024]{1,0:T(8,128)(2,1)S(1)}, bf16[128,1024]{1,0:T(8,128)(2,1)S(1)}, u32[]{:S(2)}, u32[]{:S(2)}) %collective-permute-start) | collective-permute-done | bytes 262176 | tf_op jit(solution)/shard_map/ppermute | solution.py:17
  71.2 1.2 convolution_convert_fusion
  72.5 0.7 broadcast_compare_fusion.2
  73.1 0.7 bitcast_select_fusion
  73.9 0.9 maximum_select_fusion.1
  74.8 3.6 all-to-all-start
  78.6 0.7 broadcast_compare_fusion.4
  79.2 48.9 %reduce-scatter.6.cloned.1.call-done = bf16[128,128]{0,1:T(8,128)(2,1)} async-done(((bf16[128,2048]{0,1:T(8,128)(2,1)}), bf16[128,128]{0,1:T(8,128)(2,1)}) %reduce-scatter.6.cloned.1.call-update) | async-done | bytes 32784 | tf_op jit(solution)/shard_map/reduce_scatter | solution.py:81
  128.2 0.8 fusion.38
  129.0 24.0 %all_gather.26 = bf16[128,1024]{1,0:T(8,128)(2,1)S(1)} all-gather(bf16[128,128]{1,0:T(8,128)(2,1)S(1)} %get-tuple-element.37), channel_id=1, replica_groups=mesh['leaf'=4,'row'=16,'col'=8] {'col'}, dimensions={1}, use_global_device_ids=true | all-gather | bytes 294912 | tf_op jit(solution)/shard_map/all_gather | solution.py:88
  153.0 2.6 collective-permute-start.1
  155.9 5.5 %collective-permute-done.1 = bf16[128,1024]{1,0:T(8,128)(2,1)} collective-permute-done((bf16[128,1024]{1,0:T(8,128)(2,1)S(1)}, bf16[128,1024]{1,0:T(8,128)(2,1)}, u32[]{:S(2)}, u32[]{:S(2)}) %collective-permute-start.1) | collective-permute-done | bytes 262176 | tf_op jit(solution)/shard_map/ppermute | solution.py:17
  161.4 1.2 maximum_select_fusion.2
  162.6 1.5 pad_maximum_fusion.1
  164.1 8.7 %all-gather.5.cloned.1.call-done = bf16[2,2048,256]{2,1,0:T(8,128)(2,1)} async-done(((bf16[2,128,256]{2,1,0:T(8,128)(2,1)}), bf16[2,2048,256]{2,1,0:T(8,128)(2,1)}) %all-gather.5.cloned.1.call-update) | async-done | bytes 2097168 | tf_op jit(solution)/shard_map/all_gather | solution.py:108
  172.8 3.6 fusion.6
  176.5 39.9 %all-gather.7.cloned.1.call-done = bf16[2,128,2048]{2,1,0:T(8,128)(2,1)} async-done(((bf16[2,128,256]{2,1,0:T(8,128)(2,1)}), bf16[2,128,2048]{2,1,0:T(8,128)(2,1)}) %all-gather.7.cloned.1.call-update) | async-done | bytes 1048592 | tf_op jit(solution)/shard_map/all_gather | solution.py:111
  216.5 2.8 fusion.2
  219.7 0.7 broadcast_select_fusion
  220.9 0.6 fusion.24
  222.2 0.6 fusion.22
  222.8 0.6 fusion.21
  223.5 0.6 fusion.20
  224.1 0.6 fusion.19
  224.8 0.6 fusion.18
  226.7 0.6 fusion.15
  227.3 0.6 fusion.14
  227.9 0.6 fusion.13
  228.6 0.6 fusion.12
  229.2 0.6 fusion.11
  229.8 0.6 fusion.10
  231.1 7.5 %all-to-all-start.1 = ((bf16[16,2,128,128]{3,2,1,0:T(8,128)(2,1)}), bf16[16,2,128,128]{3,2,1,0:T(8,128)(2,1)}, u32[]{:S(2)}, u32[]{:S(2)}) async-start(bf16[16,2,128,128]{3,2,1,0:T(8,128)(2,1)} %fusion.9), calls=%async_computation.3 | async-start | bytes 2097152 | tf_op jit(solution)/shard_map/all_to_all | solution.py:123
  238.9 0.7 broadcast_compare_fusion.3
  239.8 2.3 maximum_bitcast_fusion
  242.1 25.5 %all-to-all-done.1 = bf16[16,2,128,128]{3,2,1,0:T(8,128)(2,1)} async-done(((bf16[16,2,128,128]{3,2,1,0:T(8,128)(2,1)}), bf16[16,2,128,128]{3,2,1,0:T(8,128)(2,1)}, u32[]{:S(2)}, u32[]{:S(2)}) %all-to-all-start.1) | async-done | bytes 1048608 | tf_op jit(solution)/shard_map/all_to_all | solution.py:123
  267.5 2.3 copy.69
  269.9 2.3 copy.83
  272.1 15.0 %reduce-scatter.8.cloned.1.call-done = bf16[256,128]{0,1:T(8,128)(2,1)} async-done(((bf16[256,2048]{0,1:T(8,128)(2,1)}), bf16[256,128]{0,1:T(8,128)(2,1)}) %reduce-scatter.8.cloned.1.call-update) | async-done | bytes 65552 | tf_op jit(solution)/shard_map/reduce_scatter | solution.py:113
  287.1 0.9 fusion.40
  288.1 27.5 %all_gather.30 = bf16[128,2048]{1,0:T(8,128)(2,1)S(1)} all-gather(bf16[128,256]{1,0:T(8,128)(2,1)S(1)} %get-tuple-element.35), channel_id=1, replica_groups=mesh['leaf'=4,'row'=16,'col'=8] {'col'}, dimensions={1}, use_global_device_ids=true | all-gather | bytes 589824 | tf_op jit(solution)/shard_map/all_gather | solution.py:121
  315.5 1.3 maximum_bitcast_fusion.2
  316.9 3.6 pad_maximum_fusion
  320.5 17.2 %all-gather.9.cloned.1.call-done = bf16[2,4096,256]{2,1,0:T(8,128)(2,1)} async-done(((bf16[2,256,256]{2,1,0:T(8,128)(2,1)}), bf16[2,4096,256]{2,1,0:T(8,128)(2,1)}) %all-gather.9.cloned.1.call-update) | async-done | bytes 4194320 | tf_op jit(solution)/shard_map/all_gather | solution.py:153
  337.7 39.1 %scatter_custom_fusion = bf16[12288,256]{1,0:T(8,128)(2,1)} fusion(s32[8192]{0:T(1024)S(1)} %bitcast.199, bf16[8192,256]{1,0:T(8,128)(2,1)} %bitcast.200, bf16[]{:T(256)} %constant.73.clone.1), kind=kCustom, calls=%fused_computation.3 | custom fusion | bytes 6291968
  376.8 7.6 %fusion.5 = bf16[2,384,256]{1,2,0:T(8,128)(2,1)S(1)} fusion(bf16[2,6144,256]{2,1,0:T(8,128)(2,1)} %bitcast.185, bf16[384,6144,1]{1,0,2:T(8,128)(2,1)} %bitcast.187, pred[2,384]{1,0:T(4,128)(4,1)S(1)} %compare_reduce_fusion), kind=kOutput, calls=%fused_computation.15 | convolution fusion | flops 2416508928 | bytes 11404032 | tf_op jit(solution)/shard_map/ab,ebn->ean/dot_general | solution.py:159
  384.4 0.9 copy.72
  385.4 55.5 %all-gather.11.cloned.1.call-done = bf16[2,3,128,2048]{3,2,1,0:T(8,128)(2,1)} async-done(((bf16[2,3,128,256]{3,2,1,0:T(8,128)(2,1)}), bf16[2,3,128,2048]{3,2,1,0:T(8,128)(2,1)}) %all-gather.11.cloned.1.call-update) | async-done | bytes 3145744 | tf_op jit(solution)/shard_map/all_gather | solution.py:167
  440.9 3.3 bitcast_convert_fusion
  444.2 3.8 copy.84
  448.0 3.4 copy.90
  451.5 0.7 copy.74
  452.2 0.7 copy.75
  453.0 60.0 %reduce-scatter.10.cloned.1.call-done = bf16[128,512]{1,0:T(8,128)(2,1)} async-done(((bf16[2048,512]{1,0:T(8,128)(2,1)}), bf16[128,512]{1,0:T(8,128)(2,1)}) %reduce-scatter.10.cloned.1.call-update) | async-done | bytes 131088
  512.9 0.9 reshape.276
  514.0 0.8 subtract_convert_fusion
  (76 shorter events, 5.3 us)
Async XLA Ops:
  7.2 65.9 %copy-start.5 = (bf16[1,2,128,256]{3,2,1,0:T(8,128)(2,1)S(1)}, bf16[1,2,128,256]{3,2,1,0:T(8,128)(2,1)}, u32[]{:S(2)}) copy-start(bf16[1,2,128,256]{3,2,1,0:T(8,128)(2,1)} %param.14) | copy-start | bytes 393220
  7.2 121.0 %reduce-scatter.6.cloned.1.call-start = ((), (), s32[]{:S(2)}) async-start(), calls=%async_computation.5 | async-start | bytes 557056 | tf_op jit(solution)/shard_map/reduce_scatter | solution.py:81
  37.7 37.1 %copy-start.4 = (bf16[128,128]{1,0:T(8,128)(2,1)}, bf16[128,128]{1,0:T(8,128)(2,1)S(1)}, u32[]{:S(2)}) copy-start(bf16[128,128]{1,0:T(8,128)(2,1)S(1)} %fusion.7) | copy-start | bytes 98308
  62.7 15.7 %copy-start.8 = (bf16[1,128,128]{2,1,0:T(8,128)(2,1)S(1)}, bf16[1,128,128]{2,1,0:T(8,128)(2,1)}, u32[]{:S(2)}) copy-start(bf16[1,128,128]{2,1,0:T(8,128)(2,1)} %param.13) | copy-start | bytes 98308
  62.7 8.4 %collective-permute-start = (bf16[128,1024]{1,0:T(8,128)(2,1)S(1)}, bf16[128,1024]{1,0:T(8,128)(2,1)S(1)}, u32[]{:S(2)}, u32[]{:S(2)}) collective-permute-start(bf16[128,1024]{1,0:T(8,128)(2,1)S(1)} %all_gather.25), channel_id=1, source_target_pairs={{0,128},{128,0},{256,384},{384,256},{1,129},{129,1},{257,385},{385... | collective-permute-start | bytes 786440 | tf_op jit(solution)/shard_map/ppermute | solution.py:17
  72.4 100.4 %all-gather.5.cloned.1.call-start = ((), (), s32[]{:S(2)}) async-start(), calls=%async_computation.6 | async-start | bytes 2228224 | tf_op jit(solution)/shard_map/all_gather | solution.py:108
  74.8 80.9 %all-to-all-start = ((bf16[128,16,128]{2,0,1:T(8,128)(2,1)}), bf16[128,16,128]{2,0,1:T(8,128)(2,1)S(1)}, u32[]{:S(2)}, u32[]{:S(2)}) async-start(bf16[128,16,128]{2,0,1:T(8,128)(2,1)} %maximum_select_fusion.1), calls=%async_computation.1 | async-start | bytes 1048576 | tf_op jit(solution)/shard_map/all_to_all | solution.py:97
  78.4 138.1 %all-gather.7.cloned.1.call-start = ((), (), s32[]{:S(2)}) async-start(), calls=%async_computation.7 | async-start | bytes 1179648 | tf_op jit(solution)/shard_map/all_gather | solution.py:111
  153.0 8.4 %collective-permute-start.1 = (bf16[128,1024]{1,0:T(8,128)(2,1)S(1)}, bf16[128,1024]{1,0:T(8,128)(2,1)}, u32[]{:S(2)}, u32[]{:S(2)}) collective-permute-start(bf16[128,1024]{1,0:T(8,128)(2,1)S(1)} %all_gather.26), channel_id=1, source_target_pairs={{0,128},{128,0},{256,384},{384,256},{1,129},{129,1},{257,385},{385... | collective-permute-start | bytes 786440 | tf_op jit(solution)/shard_map/ppermute | solution.py:17
  162.5 1.6 copy-start.1
  164.1 52.4 %copy-start.2 = (bf16[2,128,256]{2,1,0:T(8,128)(2,1)S(1)}, bf16[2,128,256]{2,1,0:T(8,128)(2,1)}, u32[]{:S(2)}) copy-start(bf16[2,128,256]{2,1,0:T(8,128)(2,1)} %bitcast_select_fusion) | copy-start | bytes 393220
  172.8 46.6 %copy-start.12 = (s32[15]{0:T(128)S(1)}, s32[15]{0:T(128)}, u32[]{:S(2)}) copy-start(s32[15]{0:T(128)} %param.9) | copy-start | bytes 184
  172.8 46.9 %copy-start.3 = (bf16[2,256,256]{2,1,0:T(8,128)(2,1)S(1)}, bf16[2,256,256]{2,1,0:T(8,128)(2,1)}, u32[]{:S(2)}) copy-start(bf16[2,256,256]{2,1,0:T(8,128)(2,1)} %param.16) | copy-start | bytes 786436
  176.5 44.0 %copy-start.9 = (s32[2,32]{1,0:T(2,128)S(1)}, s32[2,32]{1,0:T(2,128)}, u32[]{:S(2)}) copy-start(s32[2,32]{1,0:T(2,128)} %param.10) | copy-start | bytes 772
  176.5 44.2 %copy-start.11 = (s32[2]{0:T(128)S(1)}, s32[2]{0:T(128)}, u32[]{:S(2)}) copy-start(s32[2]{0:T(128)} %constant.94) | copy-start | bytes 28
  176.5 44.3 %copy-start.10 = (s32[2]{0:T(128)S(1)}, s32[2]{0:T(128)}, u32[]{:S(2)}) copy-start(s32[2]{0:T(128)} %constant.97) | copy-start | bytes 28
  176.5 110.6 %reduce-scatter.8.cloned.1.call-start = ((), (), s32[]{:S(2)}) async-start(), calls=%async_computation.8 | async-start | bytes 1114112 | tf_op jit(solution)/shard_map/reduce_scatter | solution.py:113
  216.5 4.4 copy-start
  219.3 19.4 %copy-start.7 = (bf16[1,256,128]{2,1,0:T(8,128)(2,1)S(1)}, bf16[1,256,128]{2,1,0:T(8,128)(2,1)}, u32[]{:S(2)}) copy-start(bf16[1,256,128]{2,1,0:T(8,128)(2,1)} %param.15) | copy-start | bytes 196612
  219.4 118.3 %all-gather.9.cloned.1.call-start = ((), (), s32[]{:S(2)}) async-start(), calls=%async_computation.9 | async-start | bytes 4456448 | tf_op jit(solution)/shard_map/all_gather | solution.py:153
  231.1 36.4 %all-to-all-start.1 = ((bf16[16,2,128,128]{3,2,1,0:T(8,128)(2,1)}), bf16[16,2,128,128]{3,2,1,0:T(8,128)(2,1)}, u32[]{:S(2)}, u32[]{:S(2)}) async-start(bf16[16,2,128,128]{3,2,1,0:T(8,128)(2,1)} %fusion.9), calls=%async_computation.3 | async-start | bytes 2097152 | tf_op jit(solution)/shard_map/all_to_all | solution.py:123
  238.7 202.2 %all-gather.11.cloned.1.call-start = ((), (), s32[]{:S(2)}) async-start(), calls=%async_computation.10 | async-start | bytes 3538944 | tf_op jit(solution)/shard_map/all_gather | solution.py:167
  385.3 127.6 %reduce-scatter.10.cloned.1.call-start = ((), (), s32[]{:S(2)}) async-start(), calls=%async_computation.11 | async-start | bytes 2228224
  448.0 66.0 %copy-start.6 = (bf16[2,256,128]{2,1,0:T(8,128)(2,1)S(1)}, bf16[2,256,128]{2,1,0:T(8,128)(2,1)}, u32[]{:S(2)}) copy-start(bf16[2,256,128]{2,1,0:T(8,128)(2,1)} %param.17) | copy-start | bytes 393220
Sparse Core Ops, SparseCore 0:
  72.5 55.5 reduce-scatter.5
  131.1 41.6 all-gather.4
  176.6 39.8 all-gather.6
  219.5 67.5 reduce-scatter.7
  289.7 47.9 all-gather.8
  385.4 55.3 all-gather.10
  451.6 61.3 reduce-scatter.9
